TPU v7x, 512 devices: a whole 4x4x16 slice. The times are simulated.
512 devices in a mesh: row: 16 (over z_lo, core), col: 32 (over y, x, z_hi).
Axes of the slice: x: 4, y: 4, z: 16 (z_hi: 2, z_lo: 8; z = z_hi * 8 + z_lo), core: 2. Of those that a mesh axis runs over, the one named last changes fastest.
Arguments:
- signatures: bfloat16 [8192, 49152], P('row', 'col'), as said below
- trailing: float32 [8192, 4096], P('row', 'col'), may hold values from -6 to 6
- ridge: float32 [1], replicated, may hold values from 0.5 to 2
- panel_index: int32 [1], replicated, may hold values from 1 to 15
Outputs:
- factor: float32 [8192, 256], P(('row', 'col'))
- updated: float32 [8192, 4096], P('row', 'col')
Inputs may be any that keep to these rules, and one draw needn't show every extreme that they name: `signatures`: every diagonal block of the Gram matrix plus the ridge is positive definite.
All inputs are finite; a program needn't handle non-finite values.
Results may differ from a plain program's by a relative error of at most 0.0003.
Values may be sent and summed in bfloat16 or wider, within the bound.
No kernel may reach another device: no remote copies, remote signals or barrier semaphores. Data moves between devices by JAX's collectives and lax.ppermute only.
A program may use at most 64 MiB of HBM per device.

v0:
```python
import jax
import jax.numpy as jnp
from jax import lax
from jax.sharding import PartitionSpec as P

PANEL = 256


def spread(block, axis, owner):
    block = jnp.where(lax.axis_index(axis) == owner, block, jnp.zeros_like(block))
    return lax.psum(block, axis)


def add_ridge(block, first_row, panel_start, ridge):
    row_ids = first_row + lax.broadcasted_iota(jnp.int32, block.shape, 0)
    col_ids = panel_start + lax.broadcasted_iota(jnp.int32, block.shape, 1)
    return block + jnp.where(row_ids == col_ids, ridge[0], jnp.zeros((), block.dtype))


def mask_above(block, first_row, panel_start):
    row_ids = first_row + lax.broadcasted_iota(jnp.int32, block.shape, 0)
    return jnp.where(row_ids >= panel_start, block, jnp.zeros((), block.dtype))


def solve_rows(lower, panel_rows):
    return jax.scipy.linalg.solve_triangular(lower, panel_rows.T, lower=True).T


def local(signatures, trailing, ridge, panel_index):
    rows_dev = signatures.shape[0]
    tile_cols = trailing.shape[1]
    col_count = lax.axis_size("col")
    row_share = rows_dev // col_count
    row_pos = lax.axis_index("row")
    col_pos = lax.axis_index("col")
    panel_start = panel_index[0] * PANEL
    row_owner = panel_start // rows_dev
    local_offset = panel_start % rows_dev
    own_paths = lax.dynamic_slice_in_dim(signatures, local_offset, PANEL, 0)
    panel_paths = spread(own_paths, "row", row_owner)
    mine_rows = lax.psum_scatter(
        lax.dot_general(
            signatures, panel_paths, (((1,), (1,)), ((), ())), preferred_element_type=jnp.float32
        ),
        "col",
        scatter_dimension=0,
        tiled=True,
    )
    mine_rows = add_ridge(mine_rows, row_pos * rows_dev + col_pos * row_share, panel_start, ridge)
    source_rows = lax.all_gather(mine_rows, "col", axis=0, tiled=True)
    block_cut = lax.dynamic_slice_in_dim(source_rows, local_offset, PANEL, 0)
    diagonal = spread(block_cut, "row", row_owner)
    lower = jnp.linalg.cholesky(diagonal)
    factor_mine = solve_rows(lower, mine_rows)
    factor_mine = mask_above(factor_mine, row_pos * rows_dev + col_pos * row_share, panel_start)
    factor_block = lax.all_gather(factor_mine, "col", axis=0, tiled=True)
    window_start = panel_start + PANEL + col_pos * tile_cols
    window_owner = window_start // rows_dev
    window_cut = lax.dynamic_slice_in_dim(factor_block, window_start % rows_dev, tile_cols, 0)
    window_rows = spread(window_cut, "row", window_owner)
    updated = trailing - lax.dot_general(
        factor_block,
        window_rows,
        (((1,), (1,)), ((), ())),
        precision=lax.Precision.HIGHEST,
        preferred_element_type=jnp.float32,
    )
    return (factor_mine, updated)


def solution(mesh):
    placed = (P("row", "col"), P("row", "col"), P(), P())
    return jax.shard_map(
        local,
        mesh=mesh,
        in_specs=placed,
        out_specs=(P(("row", "col"), None), P("row", "col")),
        check_vma=False,
    )
```

profile of v0, /device:TPU:1, one launch (start us, length us, event | category | flops | bytes accessed | tf_op | source)
XLA Modules:
  0.0 1291.1 jit_solution(10216238595232170383)
XLA Ops:
  8.0 2.3 dynamic-slice_select_fusion
  10.4 204.1 %all-reduce.5.cloned.1.call-done = bf16[256,1536]{1,0:T(8,128)(2,1)} async-done(((bf16[256,1536]{1,0:T(8,128)(2,1)}), bf16[256,1536]{1,0:T(8,128)(2,1)}) %all-reduce.5.cloned.1.call-update) | async-done | bytes 786448 | tf_op jit(solution)/shard_map/psum | solution.py:11
  214.4 1.7 convolution_bitcast_fusion
  216.2 1.0 copy.18
  217.9 283.6 %reduce-scatter.4.cloned.1.call-done = f32[16,256]{1,0:T(8,128)} async-done(((f32[512,256]{1,0:T(8,128)}), f32[16,256]{1,0:T(8,128)}) %reduce-scatter.4.cloned.1.call-update) | async-done | bytes 16400
  501.6 0.8 copy.19
  502.5 137.0 %all_gather.6 = f32[512,256]{1,0:T(8,128)S(1)} all-gather(f32[16,256]{1,0:T(8,128)S(1)} %copy.11), channel_id=1, replica_groups=mesh['row'=16,'col'=32] {'col'}, dimensions={0}, use_global_device_ids=true | all-gather | bytes 540672 | tf_op jit(solution)/shard_map/all_gather | solution.py:50
  639.7 0.7 broadcast_select_fusion
  640.7 231.9 %all-reduce.7.cloned.1.call-done = f32[256,256]{0,1:T(8,128)} async-done(((f32[256,256]{0,1:T(8,128)}), f32[256,256]{0,1:T(8,128)}) %all-reduce.7.cloned.1.call-update) | async-done | bytes 262160 | tf_op jit(solution)/shard_map/psum | solution.py:11
  872.6 1.1 copy.13
  873.7 1.0 fusion
  874.7 11.7 cholesky.49
  886.4 9.8 custom-call.15
  896.7 11.7 cholesky.103
  908.8 0.6 compare_reduce_fusion
  910.9 4.4 while.1
  911.1 0.6 fusion.20
  911.6 1.4 dynamic-slice.7
  913.8 1.4 dynamic-slice.7
  915.3 19.7 %custom-call.16 = f32[2,128,128]{1,2,0:T(8,128)S(1)} custom-call(f32[2,128,128]{2,1,0:T(8,128)S(1)} %get-tuple-element.9), custom_call_target="InvertDiagBlocksLowerTriangular" | custom-call | tf_op jit(solution)/shard_map/jit(_solve_triangular)/triangular_solve | solution.py:26
  935.8 145.4 %all_gather.7 = f32[512,256]{1,0:T(8,128)S(1)} all-gather(f32[16,256]{1,0:T(8,128)S(1)} %fusion.8), channel_id=1, replica_groups=mesh['row'=16,'col'=32] {'col'}, dimensions={0}, use_global_device_ids=true | all-gather | bytes 540672 | tf_op jit(solution)/shard_map/all_gather | solution.py:56
  1081.2 0.7 dynamic-slice_select_fusion.1
  1081.9 200.4 %all-reduce.9.cloned.1.call-done = f32[128,256]{1,0:T(8,128)} async-done(((f32[128,256]{1,0:T(8,128)}), f32[128,256]{1,0:T(8,128)}) %all-reduce.9.cloned.1.call-update) | async-done | bytes 131088 | tf_op jit(solution)/shard_map/psum | solution.py:11
  1282.4 2.2 convolution_subtract_fusion
  (48 shorter events, 3.3 us)
Async XLA Ops:
  7.2 207.3 %copy-start = (bf16[512,1536]{1,0:T(8,128)(2,1)S(1)}, bf16[512,1536]{1,0:T(8,128)(2,1)}, u32[]{:S(2)}) copy-start(bf16[512,1536]{1,0:T(8,128)(2,1)} %param.4) | copy-start | bytes 4718596
  7.2 207.3 %all-reduce.5.cloned.1.call-start = ((), (), s32[]{:S(2)}) async-start(), calls=%async_computation.1 | async-start | bytes 1572864 | tf_op jit(solution)/shard_map/psum | solution.py:11
  10.3 491.2 %reduce-scatter.4.cloned.1.call-start = ((), (), s32[]{:S(2)}) async-start(), calls=%async_computation.4 | async-start | bytes 540672
  217.2 655.4 %all-reduce.7.cloned.1.call-start = ((), (), s32[]{:S(2)}) async-start(), calls=%async_computation.2 | async-start | bytes 524288 | tf_op jit(solution)/shard_map/psum | solution.py:11
  640.5 641.9 %all-reduce.9.cloned.1.call-start = ((), (), s32[]{:S(2)}) async-start(), calls=%async_computation.3 | async-start | bytes 262144 | tf_op jit(solution)/shard_map/psum | solution.py:11
  910.9 371.5 %copy-start.1 = (f32[512,128]{1,0:T(8,128)S(1)}, f32[512,128]{1,0:T(8,128)}, u32[]{:S(2)}) copy-start(f32[512,128]{1,0:T(8,128)} %param.5) | copy-start | bytes 786436
  935.8 348.7 %copy-start.2 = (f32[16,256]{1,0:T(8,128)}, f32[16,256]{1,0:T(8,128)S(1)}, u32[]{:S(2)}) copy-start(f32[16,256]{1,0:T(8,128)S(1)} %fusion.8) | copy-start | bytes 49156
Sparse Core Ops, SparseCore 0:
  10.9 203.4 all-reduce.4
  217.5 284.0 reduce-scatter.3
  640.6 231.9 all-reduce.6
  1082.0 200.2 all-reduce.8
where the time goes:
time: 1290 us
  waiting for transfers between devices  920 us (71%)
  blocking collectives  282 us (22%)
  other arithmetic  58.6 us (5%)
  between operations  16.8 us (1%)
    psum x3, waiting for transfers between devices, spread(): return lax.psum(block, axis)  636 us
    unnamed x5, waiting for transfers between devices  284 us
    all_gather x1, blocking collectives, local(): factor_block = lax.all_gather(factor_mine, 'col', axis=0, tiled=True)  145 us
    all_gather x1, blocking collectives, local(): source_rows = lax.all_gather(mine_rows, 'col', axis=0, tiled=True)  137 us
    another operation x6, other arithmetic, local(): lower = jnp.linalg.cholesky(diagonal)  34 us
  transfers between devices with their start and end apart: 4, of which 4 were waited for; matrix products, arithmetic and copies ran while one was open for 0% of the time, Pallas kernels for 0%

commit v1 on v0

--- a/solution.py
+++ b/solution.py
@@ -53,7 +53,9 @@
     lower = jnp.linalg.cholesky(diagonal)
     factor_mine = solve_rows(lower, mine_rows)
     factor_mine = mask_above(factor_mine, row_pos * rows_dev + col_pos * row_share, panel_start)
-    factor_block = lax.all_gather(factor_mine, "col", axis=0, tiled=True)
+    factor_block = jnp.concatenate(
+        lax.all_to_all(jnp.stack([factor_mine] * lax.axis_size("col")), "col", 0, 0), axis=0
+    )
     window_start = panel_start + PANEL + col_pos * tile_cols
     window_owner = window_start // rows_dev
     window_cut = lax.dynamic_slice_in_dim(factor_block, window_start % rows_dev, tile_cols, 0)

time: 1290 us -> 1170 us (0.907)
  blocking collectives: 282 us -> 137 us
    all_gather x1 -> x0, blocking collectives: 145 us -> none  [local(): factor_block = lax.all_gather(factor_mine, 'col', axis=0, tiled=True)]
    all_to_all x0 -> x1, waiting for transfers between devices: none -> 20.4 us  [local(): lax.all_to_all(jnp.stack([factor_mine] * lax.axis_size('col')), 'col', 0, 0)]
  transfers between devices with their start and end apart: 4 -> 5, of which waited for: 4 -> 5; matrix products, arithmetic and copies ran while one was open for 0% -> 0% of each run, Pallas kernels for 0% -> 0%
where the time goes in v1:
time: 1170 us
  waiting for transfers between devices  931 us (80%)
  blocking collectives  137 us (12%)
  other arithmetic  58.6 us (5%)
  between operations  16.8 us (1%)
    psum x3, waiting for transfers between devices, spread(): return lax.psum(block, axis)  627 us
    unnamed x5, waiting for transfers between devices  284 us
    all_gather x1, blocking collectives, local(): source_rows = lax.all_gather(mine_rows, 'col', axis=0, tiled=True)  137 us
    another operation x6, other arithmetic, local(): lower = jnp.linalg.cholesky(diagonal)  34 us
  transfers between devices with their start and end apart: 5, of which 5 were waited for; matrix products, arithmetic and copies ran while one was open for 0% of the time, Pallas kernels for 0%

profile of v1, /device:TPU:1, one launch (start us, length us, event | category | flops | bytes accessed | tf_op | source)
XLA Modules:
  0.0 1167.5 jit_solution(8469010676368935692)
XLA Ops:
  8.0 2.3 dynamic-slice_select_fusion
  10.4 204.1 %all-reduce.5.cloned.1.call-done = bf16[256,1536]{1,0:T(8,128)(2,1)} async-done(((bf16[256,1536]{1,0:T(8,128)(2,1)}), bf16[256,1536]{1,0:T(8,128)(2,1)}) %all-reduce.5.cloned.1.call-update) | async-done | bytes 786448 | tf_op jit(solution)/shard_map/psum | solution.py:11
  214.4 1.7 convolution_bitcast_fusion
  216.2 1.0 copy.18
  217.9 283.6 %reduce-scatter.4.cloned.1.call-done = f32[16,256]{1,0:T(8,128)} async-done(((f32[512,256]{1,0:T(8,128)}), f32[16,256]{1,0:T(8,128)}) %reduce-scatter.4.cloned.1.call-update) | async-done | bytes 16400
  501.6 0.8 copy.19
  502.5 137.0 %all_gather.3 = f32[512,256]{1,0:T(8,128)S(1)} all-gather(f32[16,256]{1,0:T(8,128)S(1)} %copy.11), channel_id=1, replica_groups=mesh['row'=16,'col'=32] {'col'}, dimensions={0}, use_global_device_ids=true | all-gather | bytes 540672 | tf_op jit(solution)/shard_map/all_gather | solution.py:50
  639.7 0.7 broadcast_select_fusion
  640.6 232.0 %all-reduce.7.cloned.1.call-done = f32[256,256]{0,1:T(8,128)} async-done(((f32[256,256]{0,1:T(8,128)}), f32[256,256]{0,1:T(8,128)}) %all-reduce.7.cloned.1.call-update) | async-done | bytes 262160 | tf_op jit(solution)/shard_map/psum | solution.py:11
  872.6 1.1 copy.13
  873.7 1.0 fusion
  874.7 11.7 %cholesky.49 = f32[128,128]{1,0:T(8,128)S(1)} custom-call(f32[128,128]{1,0:T(8,128)S(1)} %cholesky.115), custom_call_target="Cholesky" | custom-call | tf_op jit(solution)/shard_map/jit(cholesky)/cholesky | solution.py:53
  886.4 9.8 custom-call.15
  896.7 11.7 %cholesky.103 = f32[128,128]{1,0:T(8,128)S(1)} custom-call(f32[128,128]{1,0:T(8,128)S(1)} %convolution_subtract_fusion.2), custom_call_target="Cholesky" | custom-call | tf_op jit(solution)/shard_map/jit(cholesky)/cholesky | solution.py:53
  910.9 4.4 while.1
  911.6 1.4 dynamic-slice.7
  913.7 1.4 dynamic-slice.7
  915.3 19.7 %custom-call.16 = f32[2,128,128]{1,2,0:T(8,128)S(1)} custom-call(f32[2,128,128]{2,1,0:T(8,128)S(1)} %get-tuple-element.9), custom_call_target="InvertDiagBlocksLowerTriangular" | custom-call | tf_op jit(solution)/shard_map/jit(_solve_triangular)/triangular_solve | solution.py:26
  935.8 0.9 stack.2
  936.7 9.7 all-to-all-start
  946.5 20.4 %all-to-all-done = f32[32,16,256]{2,1,0:T(8,128)S(1)} async-done(((f32[32,16,256]{2,1,0:T(8,128)}), f32[32,16,256]{2,1,0:T(8,128)S(1)}, u32[]{:S(2)}, u32[]{:S(2)}) %all-to-all-start) | async-done | bytes 524320 | tf_op jit(solution)/shard_map/all_to_all | solution.py:57
  966.9 0.7 dynamic-slice_select_fusion.1
  967.6 191.2 %all-reduce.9.cloned.1.call-done = f32[128,256]{1,0:T(8,128)} async-done(((f32[128,256]{1,0:T(8,128)}), f32[128,256]{1,0:T(8,128)}) %all-reduce.9.cloned.1.call-update) | async-done | bytes 131088 | tf_op jit(solution)/shard_map/psum | solution.py:11
  1158.8 2.2 convolution_subtract_fusion
  (50 shorter events, 4.5 us)
Async XLA Ops:
  7.2 207.3 %copy-start = (bf16[512,1536]{1,0:T(8,128)(2,1)S(1)}, bf16[512,1536]{1,0:T(8,128)(2,1)}, u32[]{:S(2)}) copy-start(bf16[512,1536]{1,0:T(8,128)(2,1)} %param.4) | copy-start | bytes 4718596
  7.2 207.3 %all-reduce.5.cloned.1.call-start = ((), (), s32[]{:S(2)}) async-start(), calls=%async_computation.2 | async-start | bytes 1572864 | tf_op jit(solution)/shard_map/psum | solution.py:11
  10.3 491.2 %reduce-scatter.4.cloned.1.call-start = ((), (), s32[]{:S(2)}) async-start(), calls=%async_computation.5 | async-start | bytes 540672
  217.2 655.4 %all-reduce.7.cloned.1.call-start = ((), (), s32[]{:S(2)}) async-start(), calls=%async_computation.3 | async-start | bytes 524288 | tf_op jit(solution)/shard_map/psum | solution.py:11
  915.3 243.5 %copy-start.1 = (f32[512,128]{1,0:T(8,128)S(1)}, f32[512,128]{1,0:T(8,128)}, u32[]{:S(2)}) copy-start(f32[512,128]{1,0:T(8,128)} %param.5) | copy-start | bytes 786436
  935.8 225.1 %copy-start.2 = (f32[16,256]{1,0:T(8,128)}, f32[16,256]{1,0:T(8,128)S(1)}, u32[]{:S(2)}) copy-start(f32[16,256]{1,0:T(8,128)S(1)} %fusion.8) | copy-start | bytes 49156
  936.7 30.2 %all-to-all-start = ((f32[32,16,256]{2,1,0:T(8,128)}), f32[32,16,256]{2,1,0:T(8,128)S(1)}, u32[]{:S(2)}, u32[]{:S(2)}) async-start(f32[32,16,256]{2,1,0:T(8,128)} %stack.2), calls=%async_computation | async-start | bytes 1048576 | tf_op jit(solution)/shard_map/all_to_all | solution.py:57
  946.4 212.4 %all-reduce.9.cloned.1.call-start = ((), (), s32[]{:S(2)}) async-start(), calls=%async_computation.4 | async-start | bytes 262144 | tf_op jit(solution)/shard_map/psum | solution.py:11
Sparse Core Ops, SparseCore 0:
  10.9 203.4 all-reduce.4
  217.5 284.0 reduce-scatter.3
  640.6 231.9 all-reduce.6
  967.7 191.0 all-reduce.8

commit v2 on v0

--- a/solution.py
+++ b/solution.py
@@ -8,7 +8,7 @@
 
 def spread(block, axis, owner):
     block = jnp.where(lax.axis_index(axis) == owner, block, jnp.zeros_like(block))
-    return lax.psum(block, axis)
+    return jnp.sum(lax.all_gather(block, axis), axis=0)
 
 
 def add_ridge(block, first_row, panel_start, ridge):

time: 1290 us -> 1060 us (0.82)
  waiting for transfers between devices: 920 us -> 685 us
    psum x3 -> x0, waiting for transfers between devices: 636 us -> none  [spread(): return lax.psum(block, axis)]
    all_gather x0 -> x3, waiting for transfers between devices: none -> 401 us  [spread(): return jnp.sum(lax.all_gather(block, axis), axis=0)]
    unnamed x5 -> x4, waiting for transfers between devices: 284 us -> 0.07 us
    reduce_scatter x0 -> x1, waiting for transfers between devices: none -> 283 us  [local(): lax.psum_scatter(lax.dot_general(signatures, panel_paths, (((1,), (1,)),...]
where the time goes in v2:
time: 1060 us
  waiting for transfers between devices  685 us (65%)
  blocking collectives  280 us (26%)
  other arithmetic  70.2 us (7%)
  between operations  16.6 us (2%)
    all_gather x3, waiting for transfers between devices, spread(): return jnp.sum(lax.all_gather(block, axis), axis=0)  401 us
    reduce_scatter x1, waiting for transfers between devices, local(): lax.psum_scatter(lax.dot_general(signatures, panel_paths, (((1,), (1,)),...  283 us
    all_gather x1, blocking collectives, local(): factor_block = lax.all_gather(factor_mine, 'col', axis=0, tiled=True)  144 us
    all_gather x1, blocking collectives, local(): source_rows = lax.all_gather(mine_rows, 'col', axis=0, tiled=True)  136 us
    another operation x6, other arithmetic, local(): lower = jnp.linalg.cholesky(diagonal)  34 us
  transfers between devices with their start and end apart: 4, of which 4 were waited for; matrix products, arithmetic and copies ran while one was open for 0% of the time, Pallas kernels for 0%

profile of v2, /device:TPU:1, one launch (start us, length us, event | category | flops | bytes accessed | tf_op | source)
XLA Modules:
  0.0 1060.0 jit_solution(6581669432801921725)
XLA Ops:
  7.9 2.3 dynamic-slice_select_fusion
  10.3 151.2 %all-gather.7.cloned.1.call-done = bf16[4096,1536]{1,0:T(8,128)(2,1)} async-done(((bf16[256,1536]{1,0:T(8,128)(2,1)}), bf16[4096,1536]{1,0:T(8,128)(2,1)}) %all-gather.7.cloned.1.call-update) | async-done | bytes 12582928 | tf_op jit(solution)/shard_map/all_gather | solution.py:11
  161.4 6.9 reduce_sum.30
  168.3 1.4 convolution_bitcast_fusion
  170.5 283.4 %reduce-scatter.2.cloned.1.call-done = f32[16,256]{1,0:T(8,128)} async-done(((f32[512,256]{1,0:T(8,128)}), f32[16,256]{1,0:T(8,128)}) %reduce-scatter.2.cloned.1.call-update) | async-done | bytes 16400 | tf_op jit(solution)/shard_map/reduce_scatter | solution.py:41
  453.8 0.8 select_add_fusion
  454.6 135.6 %all_gather.26 = f32[512,256]{1,0:T(8,128)S(1)} all-gather(f32[16,256]{1,0:T(8,128)S(1)} %select_add_fusion), channel_id=1, replica_groups=mesh['row'=16,'col'=32] {'col'}, dimensions={0}, use_global_device_ids=true | all-gather | bytes 540672 | tf_op jit(solution)/shard_map/all_gather | solution.py:50
  590.3 0.7 dynamic-slice_select_fusion.1
  591.3 0.8 fusion.18
  592.1 143.0 %all-gather.9.cloned.1.call-done = f32[4096,256]{1,0:T(8,128)} async-done(((f32[256,256]{1,0:T(8,128)}), f32[4096,256]{1,0:T(8,128)}) %all-gather.9.cloned.1.call-update) | async-done | bytes 4194320 | tf_op jit(solution)/shard_map/all_gather | solution.py:11
  735.1 2.5 reduce_sum.31
  737.8 11.7 %cholesky.49 = f32[128,128]{1,0:T(8,128)S(1)} custom-call(f32[128,128]{1,0:T(8,128)S(1)} %cholesky.115), custom_call_target="Cholesky" | custom-call | tf_op jit(solution)/shard_map/jit(cholesky)/cholesky | solution.py:53
  749.5 9.8 custom-call.15
  759.8 11.7 %cholesky.103 = f32[128,128]{1,0:T(8,128)S(1)} custom-call(f32[128,128]{1,0:T(8,128)S(1)} %convolution_subtract_fusion.1), custom_call_target="Cholesky" | custom-call | tf_op jit(solution)/shard_map/jit(cholesky)/cholesky | solution.py:53
  771.6 0.7 compare_reduce_fusion
  773.8 4.3 while.1
  774.5 1.4 bitcast_dynamic-update-slice_fusion.2
  776.6 1.4 bitcast_dynamic-update-slice_fusion.2
  778.0 19.7 %custom-call.16 = f32[2,128,128]{1,2,0:T(8,128)S(1)} custom-call(f32[2,128,128]{2,1,0:T(8,128)S(1)} %get-tuple-element.9), custom_call_target="InvertDiagBlocksLowerTriangular" | custom-call | tf_op jit(solution)/shard_map/jit(_solve_triangular)/triangular_solve | solution.py:26
  798.3 144.3 %all_gather.29 = f32[512,256]{1,0:T(8,128)S(1)} all-gather(f32[16,256]{1,0:T(8,128)S(1)} %fusion.7), channel_id=1, replica_groups=mesh['row'=16,'col'=32] {'col'}, dimensions={0}, use_global_device_ids=true | all-gather | bytes 540672 | tf_op jit(solution)/shard_map/all_gather | solution.py:56
  942.6 0.7 dynamic-slice_select_fusion.2
  943.3 107.1 %all-gather.11.cloned.1.call-done = f32[2048,256]{1,0:T(8,128)} async-done(((f32[128,256]{1,0:T(8,128)}), f32[2048,256]{1,0:T(8,128)}) %all-gather.11.cloned.1.call-update) | async-done | bytes 2097168 | tf_op jit(solution)/shard_map/all_gather | solution.py:11
  1050.4 1.7 reduce_sum.32
  1052.2 1.3 convolution_subtract_fusion
  (37 shorter events, 3.1 us)
Async XLA Ops:
  7.2 154.3 %all-gather.7.cloned.1.call-start = ((), (), s32[]{:S(2)}) async-start(), calls=%async_computation.2 | async-start | bytes 13369344 | tf_op jit(solution)/shard_map/all_gather | solution.py:11
  10.2 443.6 %reduce-scatter.2.cloned.1.call-start = ((), (), s32[]{:S(2)}) async-start(), calls=%async_computation.1 | async-start | bytes 540672 | tf_op jit(solution)/shard_map/reduce_scatter | solution.py:41
  161.4 6.9 copy-start
  169.7 565.3 %all-gather.9.cloned.1.call-start = ((), (), s32[]{:S(2)}) async-start(), calls=%async_computation.3 | async-start | bytes 4456448 | tf_op jit(solution)/shard_map/all_gather | solution.py:11
  591.0 459.4 %all-gather.11.cloned.1.call-start = ((), (), s32[]{:S(2)}) async-start(), calls=%async_computation.4 | async-start | bytes 2228224 | tf_op jit(solution)/shard_map/all_gather | solution.py:11
  798.3 253.8 %copy-start.2 = (f32[16,256]{1,0:T(8,128)}, f32[16,256]{1,0:T(8,128)S(1)}, u32[]{:S(2)}) copy-start(f32[16,256]{1,0:T(8,128)S(1)} %fusion.7) | copy-start | bytes 49156
  798.3 253.8 %copy-start.1 = (f32[512,128]{1,0:T(8,128)S(1)}, f32[512,128]{1,0:T(8,128)}, u32[]{:S(2)}) copy-start(f32[512,128]{1,0:T(8,128)} %param.5) | copy-start | bytes 786436
Sparse Core Ops, SparseCore 0:
  10.3 151.0 all-gather.6
  169.9 283.9 reduce-scatter.1
  591.1 143.8 all-gather.8
  943.4 106.9 all-gather.10
